TPU v7x, 512 devices: a whole 4x8x8 slice. The times are simulated.
512 devices in a mesh: seq: 64 (over z_lo, x, y), kv: 8 (over z_hi, core).
Axes of the slice: x: 4, y: 8, z: 8 (z_hi: 4, z_lo: 2; z = z_hi * 2 + z_lo), core: 2. Of those that a mesh axis runs over, the one named last changes fastest.
Arguments:
- text_query: bfloat16 [8192, 8192], P('seq', 'kv'), may hold values from -20 to 20, as said below
- vision_key: bfloat16 [2048, 1024], P('seq', 'kv'), may hold values from -4 to 4, as said below
- vision_value: bfloat16 [2048, 1024], P('seq', 'kv'), may hold values from -6 to 6
- grad_output: bfloat16 [8192, 8192], P('seq', 'kv'), may hold values from -192 to 192
- key_weight: bfloat16 [8192, 1024], P('seq', 'kv'), may hold values from -0.1875 to 0.1875
- value_weight: bfloat16 [8192, 1024], P('seq', 'kv'), may hold values from -0.1875 to 0.1875
Outputs:
- grad_query: bfloat16 [8192, 8192], P('seq', 'kv')
- grad_vision: bfloat16 [2048, 8192], P('seq', 'kv')
Inputs may be any that keep to these rules, and one draw needn't show every extreme that they name: `text_query`: entries of order one; some rows of single heads may be large multiples of a key row. `vision_key`: entries of order one.
All inputs are finite; a program needn't handle non-finite values.
Results may differ from a plain program's by a relative error of at most 0.02.
Values may be sent and summed in bfloat16 or wider, within the bound.
A program may use at most 64 MiB of HBM per device.

v0:
```python
import math
import jax
import jax.numpy as jnp
from jax import lax
from jax.sharding import PartitionSpec as P

HEAD = 128


def sweep(block_step, running, shard_piece):
    key_part, value_part = shard_piece
    key_count = key_part.shape[0]
    block_rows = 512
    num_blocks = key_count // block_rows
    key_blocks = key_part.reshape(num_blocks, block_rows, key_part.shape[1])
    value_blocks = value_part.reshape(num_blocks, block_rows, value_part.shape[1])

    def inner(inner_state, inputs):
        key_block, value_block, block_index = inputs
        return (block_step(inner_state, key_block, value_block, block_index * block_rows), None)

    result, unused = lax.scan(
        inner, running, (key_blocks, value_blocks, jnp.arange(num_blocks, dtype=jnp.int32))
    )
    return result


def shards(text_query, vision_key, vision_value, grad_output, key_weight, value_weight):
    scaling = 1.0 / math.sqrt(HEAD)
    row_count = text_query.shape[0]
    head_count = text_query.shape[1] // HEAD
    queries = text_query.reshape(row_count, head_count, HEAD)
    upstream = grad_output.reshape(row_count, head_count, HEAD)
    shard_keys = vision_key.shape[0]
    total_keys = shard_keys * lax.axis_size("seq")

    def logit_pair(key_block, value_block):
        logits = (
            jnp.einsum("thd,kd->htk", queries, key_block, preferred_element_type=jnp.float32)
            * scaling
        )
        grad_probs = jnp.einsum(
            "thd,kd->htk", upstream, value_block, preferred_element_type=jnp.float32
        )
        return (logits, grad_probs)

    def stats_block(running, key_block, value_block, offset):
        row_max, row_sums, weighted = running
        logits, grad_probs = logit_pair(key_block, value_block)
        new_max = jnp.maximum(row_max, jnp.max(logits, axis=2))
        exponent = jnp.exp(logits - new_max[:, :, None])
        factor = jnp.exp(row_max - new_max)
        return (
            new_max,
            row_sums * factor + jnp.sum(exponent, axis=2),
            weighted * factor + jnp.sum(exponent * grad_probs, axis=2),
        )

    init_stats = (
        jnp.full((head_count, row_count), -jnp.inf, jnp.float32),
        jnp.zeros((head_count, row_count), jnp.float32),
        jnp.zeros((head_count, row_count), jnp.float32),
    )

    def make_grads(stats):
        row_max, row_sums, weighted = stats
        row_dots = weighted / row_sums

        def attend(key_block, value_block):
            logits, grad_probs = logit_pair(key_block, value_block)
            attention = jnp.exp(logits - row_max[:, :, None]) / row_sums[:, :, None]
            grad_logits = (attention * (grad_probs - row_dots[:, :, None]) * scaling).astype(
                jnp.bfloat16
            )
            return (attention, grad_logits)

        def block_terms(attention, grad_logits):
            value_term = jnp.einsum(
                "htk,thd->kd",
                attention.astype(jnp.bfloat16),
                upstream,
                preferred_element_type=jnp.float32,
            )
            key_term = jnp.einsum(
                "htk,thd->kd", grad_logits, queries, preferred_element_type=jnp.float32
            )
            return jnp.concatenate([key_term, value_term], axis=1)

        def grad_block(running, key_block, value_block, offset):
            query_grad, key_grads = running
            attention, grad_logits = attend(key_block, value_block)
            query_grad = query_grad + jnp.einsum(
                "htk,kd->thd", grad_logits, key_block, preferred_element_type=jnp.float32
            )
            key_grads = lax.dynamic_update_slice(
                key_grads, block_terms(attention, grad_logits), (offset, jnp.int32(0))
            )
            return (query_grad, key_grads)

        def query_block(query_grad, key_block, value_block, offset):
            attention, grad_logits = attend(key_block, value_block)
            return query_grad + jnp.einsum(
                "htk,kd->thd", grad_logits, key_block, preferred_element_type=jnp.float32
            )

        return (attend, block_terms, grad_block, query_block)

    init_query = jnp.zeros((row_count, head_count, HEAD), jnp.float32)
    init_grads = (init_query, jnp.zeros((total_keys, 2 * HEAD), jnp.float32))
    keys_all, values_all = (
        lax.all_gather(vision_key, "seq", axis=0, tiled=True),
        lax.all_gather(vision_value, "seq", axis=0, tiled=True),
    )
    stats = sweep(stats_block, init_stats, (keys_all, values_all))
    attend, block_terms, grad_block, query_block = make_grads(stats)
    query_grad, key_grads = sweep(grad_block, init_grads, (keys_all, values_all))
    owned_sums = lax.psum_scatter(key_grads, "seq", scatter_dimension=0, tiled=True)
    owned_grads = owned_sums.astype(jnp.bfloat16)
    merged_weights = jnp.concatenate([key_weight, value_weight], axis=1)
    vision_terms = jnp.einsum(
        "kc,rc->kr",
        owned_grads,
        lax.all_gather(merged_weights, "seq", axis=0, tiled=True),
        preferred_element_type=jnp.float32,
    )
    grad_vision = lax.psum_scatter(
        vision_terms.astype(jnp.bfloat16), "kv", scatter_dimension=1, tiled=True
    )
    grad_query = query_grad.reshape(row_count, head_count * HEAD).astype(jnp.bfloat16)
    return (grad_query, grad_vision)


def solution(mesh):
    return jax.shard_map(
        shards,
        mesh=mesh,
        in_specs=(
            P("seq", "kv"),
            P("seq", "kv"),
            P("seq", "kv"),
            P("seq", "kv"),
            P("seq", "kv"),
            P("seq", "kv"),
        ),
        out_specs=(P("seq", "kv"), P("seq", "kv")),
        check_vma=False,
    )
```

profile of v0, /device:TPU:10, one launch (start us, length us, event | category | flops | bytes accessed | tf_op | source)
XLA Modules:
  0.0 1057.6 jit_solution(18121476715610056676)
XLA Ops:
  7.3 153.0 %all_gather.9 = bf16[2048,128]{1,0:T(8,128)(2,1)} all-gather(bf16[32,128]{1,0:T(8,128)(2,1)} %param.11), channel_id=1, replica_groups=mesh['seq'=64,'kv'=8] {'seq'}, dimensions={0}, use_global_device_ids=true | all-gather | bytes 532480 | tf_op jit(solution)/shard_map/all_gather | solution.py:111
  160.2 164.7 %all_gather.10 = bf16[2048,128]{1,0:T(8,128)(2,1)} all-gather(bf16[32,128]{1,0:T(8,128)(2,1)} %param.12), channel_id=1, replica_groups=mesh['seq'=64,'kv'=8] {'seq'}, dimensions={0}, use_global_device_ids=true | all-gather | bytes 532480 | tf_op jit(solution)/shard_map/all_gather | solution.py:112
  324.9 1.1 copy.25
  326.4 0.9 copy.28
  327.2 13.4 %while.28 = (s32[]{:T(128)}, f32[8,128]{1,0:T(8,128)S(1)}, f32[8,128]{1,0:T(8,128)S(1)}, f32[8,128]{1,0:T(8,128)S(1)}, bf16[4,512,128]{2,1,0:T(8,128)(2,1)}, /*i...) while((s32[]{:T(128)}, f32[8,128]{1,0:T(8,128)S(1)}, ...), condition=%wide.region_4.5_spmd.clone, body=%wide.region_0.4_spmd.clone.sunk | while | flops 273161216 | bytes 7152752 | solution.py:22
  327.2 1.3 bitcast_reduce_fusion.2
  328.6 1.6 fusion.61
  330.6 1.3 bitcast_reduce_fusion.2
  332.0 1.6 fusion.61
  334.0 1.3 bitcast_reduce_fusion.2
  335.3 1.6 fusion.61
  337.3 1.3 bitcast_reduce_fusion.2
  338.7 1.6 fusion.61
  340.7 1.5 broadcast_in_dim.14.clone
  342.1 29.6 %while.29 = (s32[]{:T(128)}, f32[128,8,128]{0,2,1:T(8,128)S(1)}, f32[2048,256]{1,0:T(8,128)}, bf16[4,512,128]{2,1,0:T(8,128)(2,1)}, bf16[128,8,128]{0,2,1:T(8,12...) while((s32[]{:T(128)}, f32[128,8,128]{0,2,1:T(8,128)S(1)}, ...), condition=%wide.region_6.7_spmd.clone, body=%wide.region_5.6_spmd.clone.sunk | while | flops 675676160 | bytes 15611605 | solution.py:22
  342.1 1.4 fusion.74
  343.6 1.3 fusion.75
  345.4 0.5 convolution_bitcast_fusion.5
  346.1 0.6 dynamic_slice.55
  347.4 0.8 constant_dynamic-update-slice_fusion.2
  348.2 1.3 fusion.76
  349.5 1.4 fusion.74
  351.0 1.3 fusion.75
  352.3 0.5 convolution_bitcast_fusion.6
  352.8 0.5 convolution_bitcast_fusion.5
  353.5 0.6 dynamic_slice.55
  354.8 0.8 constant_dynamic-update-slice_fusion.2
  355.6 1.3 fusion.76
  356.9 1.4 fusion.74
  358.4 1.3 fusion.75
  359.7 0.5 convolution_bitcast_fusion.6
  360.2 0.5 convolution_bitcast_fusion.5
  360.9 0.6 dynamic_slice.55
  362.2 0.8 constant_dynamic-update-slice_fusion.2
  363.0 1.3 fusion.76
  364.4 1.4 fusion.74
  365.8 1.3 fusion.75
  368.4 0.6 dynamic_slice.55
  369.6 0.8 constant_dynamic-update-slice_fusion.2
  370.4 1.3 fusion.76
  371.9 0.7 copy-done.1
  372.5 0.6 pad_maximum_fusion.1
  373.2 311.3 %reduce-scatter.7.cloned.1.call-done = f32[32,256]{1,0:T(8,128)} async-done(((f32[2048,256]{1,0:T(8,128)}), f32[32,256]{1,0:T(8,128)}) %reduce-scatter.7.cloned.1.call-update) | async-done | bytes 32784
  684.6 0.9 copy.39
  685.5 308.7 %all-gather.2.cloned.1.call-done = bf16[8192,256]{1,0:T(8,128)(2,1)} async-done(((bf16[128,256]{1,0:T(8,128)(2,1)}), bf16[8192,256]{1,0:T(8,128)(2,1)}) %all-gather.2.cloned.1.call-update) | async-done | bytes 4194320 | tf_op jit(solution)/shard_map/all_gather | solution.py:123
  994.1 4.3 convolution_convert_fusion
  998.5 0.9 copy.36
  999.4 51.7 %reduce-scatter.5.cloned.1.call-done = bf16[32,1024]{1,0:T(8,128)(2,1)} async-done(((bf16[32,8192]{1,0:T(8,128)(2,1)}), bf16[32,1024]{1,0:T(8,128)(2,1)}) %reduce-scatter.5.cloned.1.call-update) | async-done | bytes 65552 | tf_op jit(solution)/shard_map/reduce_scatter | solution.py:126
  (47 shorter events, 4.5 us)
Async XLA Ops:
  7.2 319.0 %copy-start = (bf16[128,1024]{1,0:T(8,128)(2,1)S(1)}, bf16[128,1024]{1,0:T(8,128)(2,1)}, u32[]{:S(2)}) copy-start(bf16[128,1024]{1,0:T(8,128)(2,1)} %param.13) | copy-start | bytes 786436
  7.2 677.4 %reduce-scatter.7.cloned.1.call-start = ((), (), s32[]{:S(2)}) async-start(), calls=%async_computation.4 | async-start | bytes 2129920
  371.8 0.8 copy-start.1
  371.8 0.8 copy-start.2
  371.8 622.3 %all-gather.2.cloned.1.call-start = ((), (), s32[]{:S(2)}) async-start(), calls=%async_computation.2 | async-start | bytes 4259840 | tf_op jit(solution)/shard_map/all_gather | solution.py:123
  373.2 677.9 %reduce-scatter.5.cloned.1.call-start = ((), (), s32[]{:S(2)}) async-start(), calls=%async_computation.3 | async-start | bytes 589824 | tf_op jit(solution)/shard_map/reduce_scatter | solution.py:126
Sparse Core Ops, SparseCore 0:
  371.9 312.6 reduce-scatter.6
  687.4 306.6 all-gather.1
  998.6 52.4 reduce-scatter.4
where the time goes:
time: 1060 us
  waiting for transfers between devices  672 us (63%)
  blocking collectives  318 us (30%)
  matrix products  36.1 us (3%)
  between operations  13.9 us (1%)
  local copies, waits for them, and re-layouts  12.7 us (1%)
    unnamed x4, waiting for transfers between devices  311 us
    all_gather x1, waiting for transfers between devices, shards(): lax.all_gather(merged_weights, 'seq', axis=0, tiled=True)  309 us
    all_gather x1, blocking collectives, shards(): lax.all_gather(vision_value, 'seq', axis=0, tiled=True)  165 us
    all_gather x1, blocking collectives, shards(): lax.all_gather(vision_key, 'seq', axis=0, tiled=True)  153 us
    reduce_scatter x1, waiting for transfers between devices, shards(): lax.psum_scatter(vision_terms.astype(jnp.bfloat16), 'kv', scatter_dimensi...  51.7 us
  transfers between devices with their start and end apart: 3, of which 3 were waited for; matrix products, arithmetic and copies ran while one was open for 0% of the time, Pallas kernels for 0%

commit v1 on v0

--- a/solution.py
+++ b/solution.py
@@ -108,7 +108,9 @@
     init_query = jnp.zeros((row_count, head_count, HEAD), jnp.float32)
     init_grads = (init_query, jnp.zeros((total_keys, 2 * HEAD), jnp.float32))
     keys_all, values_all = (
-        lax.all_gather(vision_key, "seq", axis=0, tiled=True),
+        jnp.concatenate(
+            lax.all_to_all(jnp.stack([vision_key] * lax.axis_size("seq")), "seq", 0, 0), axis=0
+        ),
         lax.all_gather(vision_value, "seq", axis=0, tiled=True),
     )
     stats = sweep(stats_block, init_stats, (keys_all, values_all))

time: 1060 us -> 908 us (0.86)
  the two profiles are of different devices: /device:TPU:10 before, /device:TPU:4 now
where the time goes in v1:
time: 908 us; the launch traced here: 907 us
  waiting for transfers between devices  686 us (76%)
  blocking collectives  138 us (15%)
  matrix products  36.1 us (4%)
  local copies, waits for them, and re-layouts  14.4 us (2%)
  between operations  13.9 us (2%)
  starting transfers between devices  12.8 us (1%)
    unnamed x4, waiting for transfers between devices  316 us
    all_gather x1, waiting for transfers between devices, shards(): lax.all_gather(merged_weights, 'seq', axis=0, tiled=True)  309 us
    all_gather x1, blocking collectives, shards(): lax.all_gather(vision_value, 'seq', axis=0, tiled=True)  138 us
    reduce_scatter x1, waiting for transfers between devices, shards(): lax.psum_scatter(vision_terms.astype(jnp.bfloat16), 'kv', scatter_dimensi...  61.6 us
  transfers between devices with their start and end apart: 4, of which 3 were waited for; matrix products, arithmetic and copies ran while one was open for 1% of the time, Pallas kernels for 0%

profile of v1, /device:TPU:4, one launch (start us, length us, event | category | flops | bytes accessed | tf_op | source)
XLA Modules:
  0.0 907.0 jit_solution(5646922172856059942)
XLA Ops:
  7.2 1.6 stack.2
  8.8 12.6 %all-to-all-start = ((bf16[64,32,128]{2,1,0:T(8,128)(2,1)}), bf16[64,32,128]{2,1,0:T(8,128)(2,1)}, u32[]{:S(2)}, u32[]{:S(2)}) async-start(bf16[64,32,128]{2,1,0:T(8,128)(2,1)} %stack.2), calls=%async_computation | async-start | bytes 1048576 | tf_op jit(solution)/shard_map/all_to_all | solution.py:112
  21.5 1.1 copy.25
  23.0 0.9 copy.28
  23.9 138.3 %all_gather.6 = bf16[2048,128]{1,0:T(8,128)(2,1)} all-gather(bf16[32,128]{1,0:T(8,128)(2,1)S(1)} %copy-done.3), channel_id=1, replica_groups=mesh['seq'=64,'kv'=8] {'seq'}, dimensions={0}, use_global_device_ids=true | all-gather | bytes 532480 | tf_op jit(solution)/shard_map/all_gather | solution.py:114
  162.2 13.4 %while.28 = (s32[]{:T(128)}, f32[8,128]{1,0:T(8,128)S(1)}, f32[8,128]{1,0:T(8,128)S(1)}, f32[8,128]{1,0:T(8,128)S(1)}, bf16[4,512,128]{2,1,0:T(8,128)(2,1)}, /*i...) while((s32[]{:T(128)}, f32[8,128]{1,0:T(8,128)S(1)}, ...), condition=%wide.region_4.5_spmd.clone, body=%wide.region_0.4_spmd.clone.sunk | while | flops 273161216 | bytes 7152752 | solution.py:22
  162.2 1.3 bitcast_reduce_fusion.2
  163.6 1.6 fusion.61
  165.6 1.3 bitcast_reduce_fusion.2
  167.0 1.6 fusion.61
  168.9 1.3 bitcast_reduce_fusion.2
  170.3 1.6 fusion.61
  172.3 1.3 bitcast_reduce_fusion.2
  173.7 1.6 fusion.61
  175.7 1.5 broadcast_in_dim.14.clone
  177.1 29.6 %while.29 = (s32[]{:T(128)}, f32[128,8,128]{0,2,1:T(8,128)S(1)}, f32[2048,256]{1,0:T(8,128)}, bf16[4,512,128]{2,1,0:T(8,128)(2,1)}, bf16[128,8,128]{0,2,1:T(8,12...) while((s32[]{:T(128)}, f32[128,8,128]{0,2,1:T(8,128)S(1)}, ...), condition=%wide.region_6.7_spmd.clone, body=%wide.region_5.6_spmd.clone.sunk | while | flops 675676160 | bytes 15611605 | solution.py:22
  177.1 1.4 fusion.74
  178.6 1.3 fusion.75
  179.9 0.5 convolution_bitcast_fusion.6
  180.4 0.5 convolution_bitcast_fusion.5
  181.1 0.6 dynamic_slice.55
  182.4 0.9 constant_dynamic-update-slice_fusion.2
  183.2 1.3 fusion.76
  184.6 1.4 fusion.74
  186.0 1.3 fusion.75
  188.6 0.6 dynamic_slice.55
  189.8 0.8 constant_dynamic-update-slice_fusion.2
  190.6 1.3 fusion.76
  192.0 1.4 fusion.74
  193.4 1.3 fusion.75
  195.2 0.5 convolution_bitcast_fusion.5
  196.0 0.6 dynamic_slice.55
  197.2 0.9 constant_dynamic-update-slice_fusion.2
  198.1 1.3 fusion.76
  199.4 1.4 fusion.74
  200.8 1.3 fusion.75
  202.2 0.5 convolution_bitcast_fusion.6
  203.4 0.6 dynamic_slice.55
  204.6 0.8 constant_dynamic-update-slice_fusion.2
  205.5 1.3 fusion.76
  206.9 0.7 copy-done.1
  207.6 0.6 pad_maximum_fusion.1
  208.3 315.7 %reduce-scatter.7.cloned.1.call-done = f32[32,256]{1,0:T(8,128)} async-done(((f32[2048,256]{1,0:T(8,128)}), f32[32,256]{1,0:T(8,128)}) %reduce-scatter.7.cloned.1.call-update) | async-done | bytes 32784
  524.0 0.9 copy.39
  524.9 308.8 %all-gather.2.cloned.1.call-done = bf16[8192,256]{1,0:T(8,128)(2,1)} async-done(((bf16[128,256]{1,0:T(8,128)(2,1)}), bf16[8192,256]{1,0:T(8,128)(2,1)}) %all-gather.2.cloned.1.call-update) | async-done | bytes 4194320 | tf_op jit(solution)/shard_map/all_gather | solution.py:125
  833.7 4.4 convolution_convert_fusion
  838.1 0.9 copy.36
  839.0 61.6 %reduce-scatter.5.cloned.1.call-done = bf16[32,1024]{1,0:T(8,128)(2,1)} async-done(((bf16[32,8192]{1,0:T(8,128)(2,1)}), bf16[32,1024]{1,0:T(8,128)(2,1)}) %reduce-scatter.5.cloned.1.call-update) | async-done | bytes 65552 | tf_op jit(solution)/shard_map/reduce_scatter | solution.py:128
  (51 shorter events, 4.9 us)
Async XLA Ops:
  7.2 15.7 %copy-start = (bf16[128,1024]{1,0:T(8,128)(2,1)S(1)}, bf16[128,1024]{1,0:T(8,128)(2,1)}, u32[]{:S(2)}) copy-start(bf16[128,1024]{1,0:T(8,128)(2,1)} %param.13) | copy-start | bytes 786436
  7.2 16.7 %copy-start.3 = (bf16[32,128]{1,0:T(8,128)(2,1)S(1)}, bf16[32,128]{1,0:T(8,128)(2,1)}, u32[]{:S(2)}) copy-start(bf16[32,128]{1,0:T(8,128)(2,1)} %param.12) | copy-start | bytes 24580
  8.8 153.4 %all-to-all-start = ((bf16[64,32,128]{2,1,0:T(8,128)(2,1)}), bf16[64,32,128]{2,1,0:T(8,128)(2,1)}, u32[]{:S(2)}, u32[]{:S(2)}) async-start(bf16[64,32,128]{2,1,0:T(8,128)(2,1)} %stack.2), calls=%async_computation | async-start | bytes 1048576 | tf_op jit(solution)/shard_map/all_to_all | solution.py:112
  21.4 502.6 %reduce-scatter.7.cloned.1.call-start = ((), (), s32[]{:S(2)}) async-start(), calls=%async_computation.5 | async-start | bytes 2129920
  206.8 0.8 copy-start.1
  206.8 0.8 copy-start.2
  206.8 626.8 %all-gather.2.cloned.1.call-start = ((), (), s32[]{:S(2)}) async-start(), calls=%async_computation.3 | async-start | bytes 4259840 | tf_op jit(solution)/shard_map/all_gather | solution.py:125
  208.2 692.3 %reduce-scatter.5.cloned.1.call-start = ((), (), s32[]{:S(2)}) async-start(), calls=%async_computation.4 | async-start | bytes 589824 | tf_op jit(solution)/shard_map/reduce_scatter | solution.py:128
Sparse Core Ops, SparseCore 0:
  207.0 317.0 reduce-scatter.6
  526.9 306.7 all-gather.1
  838.2 62.2 reduce-scatter.4
